TPU v7x, 512 devices: a whole 4x4x16 slice. The times are simulated.
512 devices in a mesh: dom: 32 (over x, y, core), cls: 16 (over z).
Axes of the slice: x: 4, y: 4, z: 16, core: 2. Of those that a mesh axis runs over, the one named last changes fastest.
Arguments:
- images: bfloat16 [16384, 128, 128], P(('dom', 'cls')), may hold values from -6 to 6
- class_ids: int32 [16384], P(('dom', 'cls')), may hold values from 0 to 255, as said below
- shifts: int32 [16384, 2], P(('dom', 'cls')), may hold values from -16 to 16
- defocus_bins: int32 [16384], P(('dom', 'cls')), may hold values from 0 to 31
- defocus: float32 [32], replicated, may hold values from 20 to 200
- regular: float32 [128, 128], replicated, may hold values from 1 to 32
Outputs:
- class_avg: float32 [256, 128, 128], P('cls')
Inputs may be any that keep to these rules, and one draw needn't show every extreme that they name: `class_ids`: the owner of class k is k // 16. Among the 32 particles of one device exactly 8 have classes of one owner, and every other owner has at most 2 of them, exactly 2 for some; all devices with the same dom index have that same most loaded owner.
All inputs are finite; a program needn't handle non-finite values.
Results may differ from a plain program's by a relative error of at most 0.0055.
Values may be sent and summed in bfloat16 or wider, within the bound.
No kernel may reach another device: no remote copies, remote signals or barrier semaphores. Data moves between devices by JAX's collectives and lax.ppermute only.
A program may use at most 64 MiB of HBM per device.

v0:
```python
import math
import jax
import jax.numpy as jnp
from jax import lax
from jax.sharding import PartitionSpec as P

OWNED = 16
PHASE = 0.1
EPSILON = 1e-05


def hartley_tables(image_side):
    indices = jnp.arange(image_side, dtype=jnp.int32)
    product = indices[:, None] * indices[None, :] % image_side
    angles = product.astype(jnp.float32) * (2.0 * math.pi / image_side)
    return (jnp.cos(angles), jnp.sin(angles))


def frequency_squared(image_side):
    indices = jnp.arange(image_side, dtype=jnp.int32)
    signed = (
        jnp.where(indices < image_side // 2, indices, indices - image_side).astype(jnp.float32)
        / image_side
    )
    return signed[:, None] * signed[:, None] + signed[None, :] * signed[None, :]


def lookup(bins, defocus):
    levels = jnp.arange(defocus.shape[0], dtype=jnp.int32)
    return jnp.sum(jnp.where(bins[:, None] == levels[None, :], defocus[None, :], 0.0), axis=1)


def weigh(pictures, offsets, bins, defocus):
    count_rows = pictures.shape[0]
    image_side = pictures.shape[1]
    indices = jnp.arange(image_side, dtype=jnp.int32)
    source_rows = (indices[None, :] - offsets[:, 0:1]) % image_side
    source_cols = (indices[None, :] - offsets[:, 1:2]) % image_side
    row_select = (source_rows[:, :, None] == indices[None, None, :]).astype(jnp.bfloat16)
    col_select = (source_cols[:, :, None] == indices[None, None, :]).astype(jnp.bfloat16)
    shifted = jnp.einsum(
        "pij,pjk->pik", row_select, pictures, preferred_element_type=jnp.float32
    ).astype(jnp.bfloat16)
    shifted = jnp.einsum(
        "pik,plk->pil", shifted, col_select, preferred_element_type=jnp.float32
    ).astype(jnp.bfloat16)
    cosine, sine_table = hartley_tables(image_side)
    factor = 1.0 / math.sqrt(image_side)
    right_table = (
        jnp.concatenate([cosine + sine_table, cosine - sine_table], axis=1) * factor
    ).astype(jnp.bfloat16)
    left_table = (jnp.stack([cosine, sine_table]) * factor).astype(jnp.bfloat16)
    halves = jnp.dot(
        shifted.reshape(count_rows * image_side, image_side),
        right_table,
        preferred_element_type=jnp.float32,
    ).astype(jnp.bfloat16)
    halves = halves.reshape(count_rows, image_side, 2, image_side)
    spectrum = jnp.einsum("kux,pxkv->puv", left_table, halves, preferred_element_type=jnp.float32)
    ctf_values = -jnp.sin(
        lookup(bins, defocus)[:, None, None] * frequency_squared(image_side)[None] + PHASE
    )
    return (ctf_values * spectrum).astype(jnp.bfloat16).reshape(count_rows, image_side * image_side)


def body(images, class_ids, shifts, defocus_bins, defocus, regular):
    owners = lax.axis_size("cls")
    count_local = images.shape[0]
    image_side = images.shape[1]
    pixels = image_side * image_side
    capacity = min(4 * count_local // owners, count_local // 2)
    owner_of = class_ids // OWNED
    local_class = class_ids % OWNED
    member = (owner_of[:, None] == jnp.arange(owners, dtype=jnp.int32)[None, :]).astype(jnp.int32)
    before = jnp.cumsum(member, axis=0) - member
    ranked = jnp.sum(before * member, axis=1)
    slot_width = (count_local - capacity + owners - 2) // (owners - 1)
    slot_count = owners * slot_width
    target = jnp.where(ranked < slot_width, owner_of * slot_width + ranked, -1)
    matches = jnp.arange(slot_count, dtype=jnp.int32)[:, None] == target[None, :]
    filled = jnp.any(matches, axis=1)
    dispatch = matches.astype(jnp.bfloat16)

    def select_ints(selection, values):
        return jnp.sum(jnp.where(selection, values[None, :], 0), axis=1)

    slot_class = jnp.where(filled, select_ints(matches, local_class), OWNED)
    slot_bin = select_ints(matches, defocus_bins)
    payload = weigh(images, shifts, defocus_bins, defocus)
    outgoing = jnp.dot(dispatch, payload, preferred_element_type=jnp.float32).astype(jnp.bfloat16)
    outgoing = outgoing.reshape(owners, slot_width, pixels)
    labels = jnp.stack([slot_class, slot_bin], axis=1).reshape(owners, slot_width, 2)
    arrived, arrived_labels = (
        lax.all_to_all(outgoing, "cls", split_axis=0, concat_axis=0, tiled=True),
        lax.all_to_all(labels, "cls", split_axis=0, concat_axis=0, tiled=True),
    )
    arrived_rows = arrived.reshape(slot_count, pixels)
    arrived_tags = arrived_labels.reshape(slot_count, 2)
    surplus = capacity - slot_width
    extra_matches = (
        jnp.arange(surplus, dtype=jnp.int32)[:, None]
        == jnp.where(ranked >= slot_width, ranked - slot_width, -1)[None, :]
    )
    extra_filled = jnp.any(extra_matches, axis=1)
    extra_rows = jnp.dot(
        extra_matches.astype(jnp.bfloat16), payload, preferred_element_type=jnp.float32
    ).astype(jnp.bfloat16)
    extra_tags = jnp.stack(
        [
            select_ints(extra_matches, local_class),
            select_ints(extra_matches, defocus_bins),
            select_ints(extra_matches, shifts[:, 0]),
            select_ints(extra_matches, shifts[:, 1]),
            jnp.where(extra_filled, select_ints(extra_matches, owner_of), -1),
        ],
        axis=1,
    )
    gathered_rows, gathered_tags = (
        lax.all_gather(extra_rows, "cls", axis=0, tiled=True),
        lax.all_gather(extra_tags, "cls", axis=0, tiled=True),
    )
    mine = gathered_tags[:, 4] == lax.axis_index("cls")
    kept_class = jnp.where(mine, gathered_tags[:, 0], OWNED)
    arrived_rows = jnp.concatenate([arrived_rows, gathered_rows], axis=0)
    arrived_tags = jnp.concatenate(
        [arrived_tags, jnp.stack([kept_class, gathered_tags[:, 1]], axis=1)], axis=0
    )
    bin_count = defocus.shape[0]
    class_select = (jnp.arange(OWNED, dtype=jnp.int32)[:, None] == arrived_tags[None, :, 0]).astype(
        jnp.bfloat16
    )
    bin_select = (arrived_tags[:, 1:2] == jnp.arange(bin_count, dtype=jnp.int32)[None, :]).astype(
        jnp.bfloat16
    )
    numerator = jnp.dot(class_select, arrived_rows, preferred_element_type=jnp.float32)
    counts = jnp.dot(class_select, bin_select, preferred_element_type=jnp.float32)
    squared = frequency_squared(image_side).reshape(pixels)
    ctf_table = jnp.sin(defocus[:, None] * squared[None, :] + PHASE)
    ctf_table = ctf_table * ctf_table
    denominator = jnp.dot(counts, ctf_table, precision=lax.Precision.HIGHEST)
    numerator, denominator = lax.psum((numerator, denominator), "dom")
    average = numerator / (denominator + regular.reshape(1, pixels))
    cosine, sine_table = hartley_tables(image_side)
    right_table = jnp.concatenate([cosine + sine_table, cosine - sine_table], axis=1)
    left_table = jnp.stack([cosine, sine_table])
    halves = jnp.dot(
        average.reshape(OWNED * image_side, image_side),
        right_table,
        precision=lax.Precision.HIGHEST,
    )
    halves = halves.reshape(OWNED, image_side, 2, image_side)
    real_image = jnp.einsum("kux,pxkv->puv", left_table, halves, precision=lax.Precision.HIGHEST)
    power_mean = jnp.mean(real_image * real_image, axis=(1, 2), keepdims=True)
    return real_image / jnp.sqrt(power_mean + EPSILON)


def solution(mesh):
    in_specs = (
        P(("dom", "cls"), None, None),
        P(("dom", "cls")),
        P(("dom", "cls"), None),
        P(("dom", "cls")),
        P(),
        P(),
    )
    out_specs = P("cls", None, None)
    return jax.shard_map(body, mesh=mesh, in_specs=in_specs, out_specs=out_specs, check_vma=False)
```

profile of v0, /device:TPU:6, one launch (start us, length us, event | category | flops | bytes accessed | tf_op | source)
XLA Modules:
  0.0 312.1 jit_solution(7579158338892761363)
XLA Ops:
  7.1 0.7 and_select_fusion
  8.1 0.8 slice_bitcast_fusion.3
  9.0 2.4 fusion.15
  11.4 1.9 convolution_convert_fusion.2
  13.4 2.1 reshape.289
  15.8 9.2 %fusion.5 = bf16[32,128,128]{1,2,0:T(8,128)(2,1)S(1)} fusion(bf16[32,128,2,128]{3,2,1,0:T(2,128)(2,1)} %reshape.289, f32[128,128]{0,1:T(8,128)S(1)} %copy.34, f32[32]{0:T(128)S(1)} %select_reduce_fusion, f32[1,128,128]{2,1,0:T(8,128)S(1)} %get-tuple-element.32, f32[1,128,128]{2,1,0:T(8,128)S(1)} %get-tuple-element.33), kind=kOutput, calls=%fused_computation.9 | convolution fusion | flops 271155200 | bytes 3342464 | tf_op jit(solution)/shard_map/kux,pxkv->puv/dot_general | solution.py:59
  25.0 0.7 copy.36
  25.7 1.4 fusion
  27.5 0.6 copy.30
  28.1 15.2 %all-to-all-start = ((s32[16,2,2]{1,2,0:T(2,128)}), s32[16,2,2]{1,2,0:T(2,128)S(1)}, u32[]{:S(2)}, u32[]{:S(2)}) async-start(s32[16,2,2]{1,2,0:T(2,128)} %copy.30), calls=%async_computation | async-start | bytes 32768 | tf_op jit(solution)/shard_map/all_to_all | solution.py:95
  43.3 0.7 convolution_convert_fusion
  44.0 1.5 reshape.291
  45.5 10.4 %all-to-all-done = s32[16,2,2]{1,2,0:T(2,128)S(1)} async-done(((s32[16,2,2]{1,2,0:T(2,128)}), s32[16,2,2]{1,2,0:T(2,128)S(1)}, u32[]{:S(2)}, u32[]{:S(2)}) %all-to-all-start) | async-done | bytes 288 | tf_op jit(solution)/shard_map/all_to_all | solution.py:95
  55.9 3.7 %all-to-all-start.1 = ((bf16[16,2,16384]{2,1,0:T(2,128)(2,1)}), bf16[16,2,16384]{2,1,0:T(2,128)(2,1)S(1)}, u32[]{:S(2)}, u32[]{:S(2)}) async-start(bf16[16,2,16384]{2,1,0:T(2,128)(2,1)} %reshape.291), calls=%async_computation.1 | async-start | bytes 2097152 | tf_op jit(solution)/shard_map/all_to_all | solution.py:94
  60.1 82.0 %all-gather = s32[16,6,5]{2,1,0:T(8,128)S(1)} all-gather(s32[1,6,5]{2,1,0:T(8,128)S(1)} %bitcast.75), channel_id=1, replica_groups=mesh['dom'=32,'cls'=16] {'cls'}, dimensions={0}, use_global_device_ids=true | all-gather | bytes 2040 | tf_op jit(solution)/shard_map/all_gather | solution.py:120
  142.8 9.6 %fusion.8 = f32[16,16384]{1,0:T(8,128)} fusion(f32[16,32]{1,0:T(8,128)S(1)} %fusion.48, f32[16384]{0:T(1024)S(1)} %get-tuple-element.20, f32[32]{0:T(128)S(1)} %copy-done.3), kind=kOutput, calls=%fused_computation.12 | convolution fusion | flops 102236160 | bytes 1116288 | tf_op jit(solution)/shard_map/dot_general | solution.py:140
  152.4 0.4 reshape.292
  152.8 4.9 %reshape.296 = bf16[96,16384]{1,0:T(8,128)(2,1)} reshape(bf16[16,6,16384]{2,1,0:T(8,128)(2,1)} %all-gather.4.cloned.1.call-done) | data formatting | bytes 6291456
  157.7 3.5 %fusion.1 = f32[16,16384]{1,0:T(8,128)} fusion(bf16[96,16384]{1,0:T(8,128)(2,1)} %reshape.296, bf16[32,16384]{1,0:T(8,128)(2,1)S(1)} %reshape.292, s32[128]{0:T(128)S(1)} %get-tuple-element.17), kind=kOutput, calls=%fused_computation.4 | convolution fusion | flops 75499520 | bytes 5243392 | tf_op jit(solution)/shard_map/dot_general | solution.py:135
  161.3 136.9 %all-reduce.3.cloned.1.call-done = (f32[16,16384]{1,0:T(8,128)}, f32[16,16384]{1,0:T(8,128)}) async-done(((f32[16,16384]{1,0:T(8,128)}, f32[16,16384]{1,0:T(8,128)}), (f32[16,16384]{1,0:T(8,128)}, f32[16,16384]{1,0:T(8,128)})) %all-reduce.3.cloned.1.call-update) | async-done | bytes 2097168 | tf_op jit(solution)/shard_map/psum | solution.py:141
  298.1 1.7 divide_bitcast_fusion.1
  300.0 1.8 fusion.21
  301.9 1.9 multiply_reduce_fusion
  303.9 1.3 copy.38
  (48 shorter events, 3.3 us)
Async XLA Ops:
  6.5 2.4 copy-start
  6.5 146.3 %all-gather.4.cloned.1.call-start = ((), (), s32[]{:S(2)}) async-start(), calls=%async_computation.2 | async-start | bytes 4456448 | tf_op jit(solution)/shard_map/all_gather | solution.py:119
  13.3 2.3 copy-start.2
  13.3 2.3 copy-start.3
  28.1 27.8 %all-to-all-start = ((s32[16,2,2]{1,2,0:T(2,128)}), s32[16,2,2]{1,2,0:T(2,128)S(1)}, u32[]{:S(2)}, u32[]{:S(2)}) async-start(s32[16,2,2]{1,2,0:T(2,128)} %copy.30), calls=%async_computation | async-start | bytes 32768 | tf_op jit(solution)/shard_map/all_to_all | solution.py:95
  55.9 96.4 %all-to-all-start.1 = ((bf16[16,2,16384]{2,1,0:T(2,128)(2,1)}), bf16[16,2,16384]{2,1,0:T(2,128)(2,1)S(1)}, u32[]{:S(2)}, u32[]{:S(2)}) async-start(bf16[16,2,16384]{2,1,0:T(2,128)(2,1)} %reshape.291), calls=%async_computation.1 | async-start | bytes 2097152 | tf_op jit(solution)/shard_map/all_to_all | solution.py:94
  59.6 238.6 %all-reduce.3.cloned.1.call-start = ((), (), s32[]{:S(2)}) async-start(), calls=%async_computation.3 | async-start | bytes 4194304 | tf_op jit(solution)/shard_map/psum | solution.py:141
  161.2 136.9 %copy-start.1 = (f32[128,128]{1,0:T(8,128)S(1)}, f32[128,128]{1,0:T(8,128)}, u32[]{:S(2)}) copy-start(f32[128,128]{1,0:T(8,128)} %param.11) | copy-start | bytes 196612
Sparse Core Ops, SparseCore 0:
  27.2 124.3 all-gather.3
  161.4 136.7 all-reduce.2
where the time goes:
time: 313 us; the launch traced here: 312 us
  waiting for transfers between devices  147 us (47%)
  blocking collectives  82 us (26%)
  matrix products  32.6 us (10%)
  starting transfers between devices  18.9 us (6%)
  between operations  13.6 us (4%)
  local copies, waits for them, and re-layouts  13.3 us (4%)
  other arithmetic  4.4 us (1%)
    psum x1, waiting for transfers between devices, body(): numerator, denominator = lax.psum((numerator, denominator), 'dom')  137 us
    all_gather x1, blocking collectives, body(): lax.all_gather(extra_tags, 'cls', axis=0, tiled=True)  82 us
    all_to_all x1, starting transfers between devices, body(): lax.all_to_all(labels, 'cls', split_axis=0, concat_axis=0, tiled=True)  15.2 us
    all_to_all x1, waiting for transfers between devices, body(): lax.all_to_all(labels, 'cls', split_axis=0, concat_axis=0, tiled=True)  10.4 us
    dot_general x1, matrix products, body(): denominator = jnp.dot(counts, ctf_table, precision=lax.Precision.HIGHEST)  9.57 us
    dot_general x1, matrix products, weigh(): jnp.einsum('kux,pxkv->puv', left_table, halves, preferred_element_type=jn...  9.16 us
  transfers between devices with their start and end apart: 4, of which 2 were waited for; matrix products, arithmetic and copies ran while one was open for 5% of the time, Pallas kernels for 0%

commit v1 on v0

--- a/solution.py
+++ b/solution.py
@@ -7,6 +7,27 @@
 OWNED = 16
 PHASE = 0.1
 EPSILON = 1e-05
+
+
+def collect(value, axis, dim):
+    size, index, extent = (lax.axis_size(axis), lax.axis_index(axis), value.shape[dim])
+    right = [(i, (i + 1) % size) for i in range(size)]
+    left = [(i, (i - 1) % size) for i in range(size)]
+    out = jnp.zeros((*value.shape[:dim], size * extent, *value.shape[dim + 1 :]), value.dtype)
+    out = lax.dynamic_update_slice_in_dim(out, value, index * extent, axis=dim)
+    from_left = from_right = value
+    middle = size // 2
+    for turn in range(1, middle + 1):
+        from_left = lax.ppermute(from_left, axis, right)
+        out = lax.dynamic_update_slice_in_dim(
+            out, from_left, (index - turn) % size * extent, axis=dim
+        )
+        if turn < size - middle:
+            from_right = lax.ppermute(from_right, axis, left)
+            out = lax.dynamic_update_slice_in_dim(
+                out, from_right, (index + turn) % size * extent, axis=dim
+            )
+    return out
 
 
 def hartley_tables(image_side):
@@ -117,7 +138,7 @@
     )
     gathered_rows, gathered_tags = (
         lax.all_gather(extra_rows, "cls", axis=0, tiled=True),
-        lax.all_gather(extra_tags, "cls", axis=0, tiled=True),
+        collect(extra_tags, "cls", 0),
     )
     mine = gathered_tags[:, 4] == lax.axis_index("cls")
     kept_class = jnp.where(mine, gathered_tags[:, 0], OWNED)

time: 313 us -> 341 us (1.089)
  blocking collectives: 82 us -> 0 us
  waiting for transfers between devices: 147 us -> 202 us
  starting transfers between devices: 18.9 us -> 70.3 us
  local copies, waits for them, and re-layouts: 13.3 us -> 16.9 us
    all_gather x1 -> x0, blocking collectives: 82 us -> none  [body(): lax.all_gather(extra_tags, 'cls', axis=0, tiled=True)]
    ppermute x0 -> x15, waiting for transfers between devices: none -> 53.2 us  [the longest x8 53.2 us: collect(): from_left = lax.ppermute(from_left, axis, right)]
    ppermute x0 -> x15, starting transfers between devices: none -> 51.5 us  [the longest x7 32.7 us: collect(): from_right = lax.ppermute(from_right, axis, left)]
    dynamic_update_slice x0 -> x16, local copies, waits for them, and re-layouts: none -> 4.07 us  [the longest x8 2.12 us: collect(): lax.dynamic_update_slice_in_dim(out, from_left, (index - turn) % size * e...]
  transfers between devices with their start and end apart: 4 -> 19, of which waited for: 2 -> 4; matrix products, arithmetic and copies ran while one was open for 5% -> 5% of each run, Pallas kernels for 0% -> 0%
where the time goes in v1:
time: 341 us; the launch traced here: 340 us
  waiting for transfers between devices  202 us (59%)
  starting transfers between devices  70.3 us (21%)
  matrix products  32.6 us (10%)
  local copies, waits for them, and re-layouts  16.9 us (5%)
  between operations  14.2 us (4%)
  other arithmetic  3.75 us (1%)
    psum x1, waiting for transfers between devices, body(): numerator, denominator = lax.psum((numerator, denominator), 'dom')  139 us
    ppermute x8, waiting for transfers between devices, collect(): from_left = lax.ppermute(from_left, axis, right)  53.2 us
    ppermute x7, starting transfers between devices, collect(): from_right = lax.ppermute(from_right, axis, left)  32.7 us
    ppermute x8, starting transfers between devices, collect(): from_left = lax.ppermute(from_left, axis, right)  18.8 us
    all_to_all x1, starting transfers between devices, body(): lax.all_to_all(labels, 'cls', split_axis=0, concat_axis=0, tiled=True)  15.2 us
    all_to_all x1, waiting for transfers between devices, body(): lax.all_to_all(labels, 'cls', split_axis=0, concat_axis=0, tiled=True)  10.4 us
    dot_general x1, matrix products, body(): denominator = jnp.dot(counts, ctf_table, precision=lax.Precision.HIGHEST)  9.56 us
    dot_general x1, matrix products, weigh(): jnp.einsum('kux,pxkv->puv', left_table, halves, preferred_element_type=jn...  9.16 us
  transfers between devices with their start and end apart: 19, of which 4 were waited for; matrix products, arithmetic and copies ran while one was open for 5% of the time, Pallas kernels for 0%

profile of v1, /device:TPU:6, one launch (start us, length us, event | category | flops | bytes accessed | tf_op | source)
XLA Modules:
  0.0 340.3 jit_solution(14037906753523479011)
XLA Ops:
  8.0 2.4 fusion.15
  10.4 1.9 convolution_convert_fusion.2
  12.4 2.1 reshape.289
  14.8 9.2 %fusion.5 = bf16[32,128,128]{1,2,0:T(8,128)(2,1)S(1)} fusion(bf16[32,128,2,128]{3,2,1,0:T(2,128)(2,1)} %reshape.289, f32[128,128]{0,1:T(8,128)S(1)} %copy.24, f32[32]{0:T(128)S(1)} %select_reduce_fusion, f32[1,128,128]{2,1,0:T(8,128)S(1)} %get-tuple-element.32, f32[1,128,128]{2,1,0:T(8,128)S(1)} %get-tuple-element.33), kind=kOutput, calls=%fused_computation.9 | convolution fusion | flops 271155200 | bytes 3342464 | tf_op jit(solution)/shard_map/kux,pxkv->puv/dot_general | solution.py:80
  27.5 15.2 %all-to-all-start = ((s32[16,2,2]{1,2,0:T(2,128)}), s32[16,2,2]{1,2,0:T(2,128)S(1)}, u32[]{:S(2)}, u32[]{:S(2)}) async-start(s32[16,2,2]{1,2,0:T(2,128)} %copy.22), calls=%async_computation | async-start | bytes 32768 | tf_op jit(solution)/shard_map/all_to_all | solution.py:116
  44.9 10.4 %all-to-all-done = s32[16,2,2]{1,2,0:T(2,128)S(1)} async-done(((s32[16,2,2]{1,2,0:T(2,128)}), s32[16,2,2]{1,2,0:T(2,128)S(1)}, u32[]{:S(2)}, u32[]{:S(2)}) %all-to-all-start) | async-done | bytes 288 | tf_op jit(solution)/shard_map/all_to_all | solution.py:116
  55.3 3.7 %all-to-all-start.1 = ((bf16[16,2,16384]{2,1,0:T(2,128)(2,1)}), bf16[16,2,16384]{2,1,0:T(2,128)(2,1)S(1)}, u32[]{:S(2)}, u32[]{:S(2)}) async-start(bf16[16,2,16384]{2,1,0:T(2,128)(2,1)} %reshape.291), calls=%async_computation.1 | async-start | bytes 2097152 | tf_op jit(solution)/shard_map/all_to_all | solution.py:115
  59.3 3.7 %collective-permute-start = (s32[6,5]{0,1:T(8,128)S(1)}, s32[6,5]{0,1:T(8,128)S(1)}, u32[]{:S(2)}, u32[]{:S(2)}) collective-permute-start(s32[6,5]{0,1:T(8,128)S(1)} %stack.41), channel_id=1, source_target_pairs={{0,1},{1,2},{2,3},{3,4},{4,5},{5,6},{6,7},{7,8},{8,9},{9,10},{10,1... | collective-permute-start | bytes 368 | tf_op jit(solution)/shard_map/ppermute | solution.py:21
  63.1 3.3 collective-permute-start.1
  67.0 49.1 %collective-permute-done = s32[6,5]{0,1:T(8,128)S(1)} collective-permute-done((s32[6,5]{0,1:T(8,128)S(1)}, s32[6,5]{0,1:T(8,128)S(1)}, u32[]{:S(2)}, u32[]{:S(2)}) %collective-permute-start) | collective-permute-done | bytes 152 | tf_op jit(solution)/shard_map/ppermute | solution.py:21
  116.1 3.3 collective-permute-start.2
  119.4 3.7 %collective-permute-start.3 = (s32[6,5]{0,1:T(8,128)S(1)}, s32[6,5]{0,1:T(8,128)S(1)}, u32[]{:S(2)}, u32[]{:S(2)}) collective-permute-start(s32[6,5]{0,1:T(8,128)S(1)} %collective-permute-done.1), channel_id=1, source_target_pairs={{0,15},{1,0},{2,1},{3,2},{4,3},{5,4},{6,5},{7,6},{8,7},{9,8},{10,9... | collective-permute-start | bytes 368 | tf_op jit(solution)/shard_map/ppermute | solution.py:26
  123.7 2.1 collective-permute-start.4
  125.8 4.9 %collective-permute-start.5 = (s32[6,5]{0,1:T(8,128)S(1)}, s32[6,5]{0,1:T(8,128)S(1)}, u32[]{:S(2)}, u32[]{:S(2)}) collective-permute-start(s32[6,5]{0,1:T(8,128)S(1)} %collective-permute-done.3), channel_id=1, source_target_pairs={{0,15},{1,0},{2,1},{3,2},{4,3},{5,4},{6,5},{7,6},{8,7},{9,8},{10,9... | collective-permute-start | bytes 368 | tf_op jit(solution)/shard_map/ppermute | solution.py:26
  133.2 5.1 %collective-permute-start.7 = (s32[6,5]{0,1:T(8,128)S(1)}, s32[6,5]{0,1:T(8,128)S(1)}, u32[]{:S(2)}, u32[]{:S(2)}) collective-permute-start(s32[6,5]{0,1:T(8,128)S(1)} %collective-permute-done.5), channel_id=1, source_target_pairs={{0,15},{1,0},{2,1},{3,2},{4,3},{5,4},{6,5},{7,6},{8,7},{9,8},{10,9... | collective-permute-start | bytes 368 | tf_op jit(solution)/shard_map/ppermute | solution.py:26
  140.8 5.1 %collective-permute-start.9 = (s32[6,5]{0,1:T(8,128)S(1)}, s32[6,5]{0,1:T(8,128)S(1)}, u32[]{:S(2)}, u32[]{:S(2)}) collective-permute-start(s32[6,5]{0,1:T(8,128)S(1)} %collective-permute-done.7), channel_id=1, source_target_pairs={{0,15},{1,0},{2,1},{3,2},{4,3},{5,4},{6,5},{7,6},{8,7},{9,8},{10,9... | collective-permute-start | bytes 368 | tf_op jit(solution)/shard_map/ppermute | solution.py:26
  148.4 5.1 %collective-permute-start.11 = (s32[6,5]{0,1:T(8,128)S(1)}, s32[6,5]{0,1:T(8,128)S(1)}, u32[]{:S(2)}, u32[]{:S(2)}) collective-permute-start(s32[6,5]{0,1:T(8,128)S(1)} %collective-permute-done.9), channel_id=1, source_target_pairs={{0,15},{1,0},{2,1},{3,2},{4,3},{5,4},{6,5},{7,6},{8,7},{9,8},{10,9... | collective-permute-start | bytes 368 | tf_op jit(solution)/shard_map/ppermute | solution.py:26
  154.1 1.9 collective-permute-start.12
  156.0 5.3 %collective-permute-start.13 = (s32[6,5]{0,1:T(8,128)S(1)}, s32[6,5]{0,1:T(8,128)S(1)}, u32[]{:S(2)}, u32[]{:S(2)}) collective-permute-start(s32[6,5]{0,1:T(8,128)S(1)} %collective-permute-done.11), channel_id=1, source_target_pairs={{0,15},{1,0},{2,1},{3,2},{4,3},{5,4},{6,5},{7,6},{8,7},{9,8},{10,9... | collective-permute-start | bytes 368 | tf_op jit(solution)/shard_map/ppermute | solution.py:26
  164.5 4.1 %collective-permute-done.14 = s32[6,5]{0,1:T(8,128)S(1)} collective-permute-done((s32[6,5]{0,1:T(8,128)S(1)}, s32[6,5]{0,1:T(8,128)S(1)}, u32[]{:S(2)}, u32[]{:S(2)}) %collective-permute-start.14) | collective-permute-done | bytes 152 | tf_op jit(solution)/shard_map/ppermute | solution.py:21
  169.1 9.6 %fusion.8 = f32[16,16384]{1,0:T(8,128)} fusion(f32[16,32]{1,0:T(8,128)S(1)} %fusion.48, f32[16384]{0:T(1024)S(1)} %get-tuple-element.20, f32[32]{0:T(128)S(1)} %copy-done.4), kind=kOutput, calls=%fused_computation.12 | convolution fusion | flops 102236160 | bytes 1116288 | tf_op jit(solution)/shard_map/dot_general | solution.py:161
  179.1 4.9 %reshape.294 = bf16[96,16384]{1,0:T(8,128)(2,1)} reshape(bf16[16,6,16384]{2,1,0:T(8,128)(2,1)} %all-gather.3.cloned.1.call-done) | data formatting | bytes 6291456
  184.0 3.5 %fusion.1 = f32[16,16384]{1,0:T(8,128)} fusion(bf16[96,16384]{1,0:T(8,128)(2,1)} %reshape.294, bf16[32,16384]{1,0:T(8,128)(2,1)S(1)} %reshape.292, s32[128]{0:T(128)S(1)} %get-tuple-element.17), kind=kOutput, calls=%fused_computation.4 | convolution fusion | flops 75499520 | bytes 5243392 | tf_op jit(solution)/shard_map/dot_general | solution.py:156
  187.6 138.8 %all-reduce.3.cloned.1.call-done = (f32[16,16384]{1,0:T(8,128)}, f32[16,16384]{1,0:T(8,128)}) async-done(((f32[16,16384]{1,0:T(8,128)}, f32[16,16384]{1,0:T(8,128)}), (f32[16,16384]{1,0:T(8,128)}, f32[16,16384]{1,0:T(8,128)})) %all-reduce.3.cloned.1.call-update) | async-done | bytes 2097168 | tf_op jit(solution)/shard_map/psum | solution.py:162
  (93 shorter events, 27.5 us)
Async XLA Ops:
  6.5 1.4 copy-start
  6.5 172.5 %all-gather.3.cloned.1.call-start = ((), (), s32[]{:S(2)}) async-start(), calls=%async_computation.2 | async-start | bytes 4456448 | tf_op jit(solution)/shard_map/all_gather | solution.py:140
  12.4 2.3 copy-start.2
  12.4 2.3 copy-start.4
  24.0 0.7 copy-start.3
  27.5 27.8 %all-to-all-start = ((s32[16,2,2]{1,2,0:T(2,128)}), s32[16,2,2]{1,2,0:T(2,128)S(1)}, u32[]{:S(2)}, u32[]{:S(2)}) async-start(s32[16,2,2]{1,2,0:T(2,128)} %copy.22), calls=%async_computation | async-start | bytes 32768 | tf_op jit(solution)/shard_map/all_to_all | solution.py:116
  55.3 123.3 %all-to-all-start.1 = ((bf16[16,2,16384]{2,1,0:T(2,128)(2,1)}), bf16[16,2,16384]{2,1,0:T(2,128)(2,1)S(1)}, u32[]{:S(2)}, u32[]{:S(2)}) async-start(bf16[16,2,16384]{2,1,0:T(2,128)(2,1)} %reshape.291), calls=%async_computation.1 | async-start | bytes 2097152 | tf_op jit(solution)/shard_map/all_to_all | solution.py:115
  59.0 267.4 %all-reduce.3.cloned.1.call-start = ((), (), s32[]{:S(2)}) async-start(), calls=%async_computation.3 | async-start | bytes 4194304 | tf_op jit(solution)/shard_map/psum | solution.py:162
  59.3 56.7 %collective-permute-start = (s32[6,5]{0,1:T(8,128)S(1)}, s32[6,5]{0,1:T(8,128)S(1)}, u32[]{:S(2)}, u32[]{:S(2)}) collective-permute-start(s32[6,5]{0,1:T(8,128)S(1)} %stack.41), channel_id=1, source_target_pairs={{0,1},{1,2},{2,3},{3,4},{4,5},{5,6},{6,7},{7,8},{8,9},{9,10},{10,1... | collective-permute-start | bytes 368 | tf_op jit(solution)/shard_map/ppermute | solution.py:21
  63.1 56.4 %collective-permute-start.1 = (s32[6,5]{0,1:T(8,128)S(1)}, s32[6,5]{0,1:T(8,128)S(1)}, u32[]{:S(2)}, u32[]{:S(2)}) collective-permute-start(s32[6,5]{0,1:T(8,128)S(1)} %stack.41), channel_id=1, source_target_pairs={{0,15},{1,0},{2,1},{3,2},{4,3},{5,4},{6,5},{7,6},{8,7},{9,8},{10,9... | collective-permute-start | bytes 368 | tf_op jit(solution)/shard_map/ppermute | solution.py:26
  116.1 7.6 %collective-permute-start.2 = (s32[6,5]{0,1:T(8,128)S(1)}, s32[6,5]{0,1:T(8,128)S(1)}, u32[]{:S(2)}, u32[]{:S(2)}) collective-permute-start(s32[6,5]{0,1:T(8,128)S(1)} %collective-permute-done), channel_id=1, source_target_pairs={{0,1},{1,2},{2,3},{3,4},{4,5},{5,6},{6,7},{7,8},{8,9},{9,10},{10,1... | collective-permute-start | bytes 368 | tf_op jit(solution)/shard_map/ppermute | solution.py:21
  119.4 6.4 %collective-permute-start.3 = (s32[6,5]{0,1:T(8,128)S(1)}, s32[6,5]{0,1:T(8,128)S(1)}, u32[]{:S(2)}, u32[]{:S(2)}) collective-permute-start(s32[6,5]{0,1:T(8,128)S(1)} %collective-permute-done.1), channel_id=1, source_target_pairs={{0,15},{1,0},{2,1},{3,2},{4,3},{5,4},{6,5},{7,6},{8,7},{9,8},{10,9... | collective-permute-start | bytes 368 | tf_op jit(solution)/shard_map/ppermute | solution.py:26
  123.7 7.6 %collective-permute-start.4 = (s32[6,5]{0,1:T(8,128)S(1)}, s32[6,5]{0,1:T(8,128)S(1)}, u32[]{:S(2)}, u32[]{:S(2)}) collective-permute-start(s32[6,5]{0,1:T(8,128)S(1)} %collective-permute-done.2), channel_id=1, source_target_pairs={{0,1},{1,2},{2,3},{3,4},{4,5},{5,6},{6,7},{7,8},{8,9},{9,10},{10,1... | collective-permute-start | bytes 368 | tf_op jit(solution)/shard_map/ppermute | solution.py:21
  125.8 7.4 %collective-permute-start.5 = (s32[6,5]{0,1:T(8,128)S(1)}, s32[6,5]{0,1:T(8,128)S(1)}, u32[]{:S(2)}, u32[]{:S(2)}) collective-permute-start(s32[6,5]{0,1:T(8,128)S(1)} %collective-permute-done.3), channel_id=1, source_target_pairs={{0,15},{1,0},{2,1},{3,2},{4,3},{5,4},{6,5},{7,6},{8,7},{9,8},{10,9... | collective-permute-start | bytes 368 | tf_op jit(solution)/shard_map/ppermute | solution.py:26
  131.3 7.6 %collective-permute-start.6 = (s32[6,5]{0,1:T(8,128)S(1)}, s32[6,5]{0,1:T(8,128)S(1)}, u32[]{:S(2)}, u32[]{:S(2)}) collective-permute-start(s32[6,5]{0,1:T(8,128)S(1)} %collective-permute-done.4), channel_id=1, source_target_pairs={{0,1},{1,2},{2,3},{3,4},{4,5},{5,6},{6,7},{7,8},{8,9},{9,10},{10,1... | collective-permute-start | bytes 368 | tf_op jit(solution)/shard_map/ppermute | solution.py:21
  133.2 7.6 %collective-permute-start.7 = (s32[6,5]{0,1:T(8,128)S(1)}, s32[6,5]{0,1:T(8,128)S(1)}, u32[]{:S(2)}, u32[]{:S(2)}) collective-permute-start(s32[6,5]{0,1:T(8,128)S(1)} %collective-permute-done.5), channel_id=1, source_target_pairs={{0,15},{1,0},{2,1},{3,2},{4,3},{5,4},{6,5},{7,6},{8,7},{9,8},{10,9... | collective-permute-start | bytes 368 | tf_op jit(solution)/shard_map/ppermute | solution.py:26
  138.9 7.6 %collective-permute-start.8 = (s32[6,5]{0,1:T(8,128)S(1)}, s32[6,5]{0,1:T(8,128)S(1)}, u32[]{:S(2)}, u32[]{:S(2)}) collective-permute-start(s32[6,5]{0,1:T(8,128)S(1)} %collective-permute-done.6), channel_id=1, source_target_pairs={{0,1},{1,2},{2,3},{3,4},{4,5},{5,6},{6,7},{7,8},{8,9},{9,10},{10,1... | collective-permute-start | bytes 368 | tf_op jit(solution)/shard_map/ppermute | solution.py:21
  140.8 7.6 %collective-permute-start.9 = (s32[6,5]{0,1:T(8,128)S(1)}, s32[6,5]{0,1:T(8,128)S(1)}, u32[]{:S(2)}, u32[]{:S(2)}) collective-permute-start(s32[6,5]{0,1:T(8,128)S(1)} %collective-permute-done.7), channel_id=1, source_target_pairs={{0,15},{1,0},{2,1},{3,2},{4,3},{5,4},{6,5},{7,6},{8,7},{9,8},{10,9... | collective-permute-start | bytes 368 | tf_op jit(solution)/shard_map/ppermute | solution.py:26
  146.5 7.6 %collective-permute-start.10 = (s32[6,5]{0,1:T(8,128)S(1)}, s32[6,5]{0,1:T(8,128)S(1)}, u32[]{:S(2)}, u32[]{:S(2)}) collective-permute-start(s32[6,5]{0,1:T(8,128)S(1)} %collective-permute-done.8), channel_id=1, source_target_pairs={{0,1},{1,2},{2,3},{3,4},{4,5},{5,6},{6,7},{7,8},{8,9},{9,10},{10,1... | collective-permute-start | bytes 368 | tf_op jit(solution)/shard_map/ppermute | solution.py:21
  148.4 7.6 %collective-permute-start.11 = (s32[6,5]{0,1:T(8,128)S(1)}, s32[6,5]{0,1:T(8,128)S(1)}, u32[]{:S(2)}, u32[]{:S(2)}) collective-permute-start(s32[6,5]{0,1:T(8,128)S(1)} %collective-permute-done.9), channel_id=1, source_target_pairs={{0,15},{1,0},{2,1},{3,2},{4,3},{5,4},{6,5},{7,6},{8,7},{9,8},{10,9... | collective-permute-start | bytes 368 | tf_op jit(solution)/shard_map/ppermute | solution.py:26
  154.1 7.8 %collective-permute-start.12 = (s32[6,5]{0,1:T(8,128)S(1)}, s32[6,5]{0,1:T(8,128)S(1)}, u32[]{:S(2)}, u32[]{:S(2)}) collective-permute-start(s32[6,5]{0,1:T(8,128)S(1)} %collective-permute-done.10), channel_id=1, source_target_pairs={{0,1},{1,2},{2,3},{3,4},{4,5},{5,6},{6,7},{7,8},{8,9},{9,10},{10,1... | collective-permute-start | bytes 368 | tf_op jit(solution)/shard_map/ppermute | solution.py:21
  156.0 8.1 %collective-permute-start.13 = (s32[6,5]{0,1:T(8,128)S(1)}, s32[6,5]{0,1:T(8,128)S(1)}, u32[]{:S(2)}, u32[]{:S(2)}) collective-permute-start(s32[6,5]{0,1:T(8,128)S(1)} %collective-permute-done.11), channel_id=1, source_target_pairs={{0,15},{1,0},{2,1},{3,2},{4,3},{5,4},{6,5},{7,6},{8,7},{9,8},{10,9... | collective-permute-start | bytes 368 | tf_op jit(solution)/shard_map/ppermute | solution.py:26
  161.9 6.7 %collective-permute-start.14 = (s32[6,5]{0,1:T(8,128)S(1)}, s32[6,5]{0,1:T(8,128)S(1)}, u32[]{:S(2)}, u32[]{:S(2)}) collective-permute-start(s32[6,5]{0,1:T(8,128)S(1)} %collective-permute-done.12), channel_id=1, source_target_pairs={{0,1},{1,2},{2,3},{3,4},{4,5},{5,6},{6,7},{7,8},{8,9},{9,10},{10,1... | collective-permute-start | bytes 368 | tf_op jit(solution)/shard_map/ppermute | solution.py:21
  187.5 138.8 %copy-start.1 = (f32[128,128]{1,0:T(8,128)S(1)}, f32[128,128]{1,0:T(8,128)}, u32[]{:S(2)}) copy-start(f32[128,128]{1,0:T(8,128)} %param.11) | copy-start | bytes 196612
Sparse Core Ops, SparseCore 0:
  26.6 124.3 all-gather.2
  187.7 138.6 all-reduce.2
